TPU v7x, 256 devices: a whole 4x4x8 slice. The times are simulated.
256 devices in a mesh: mode: 64 (over z, y, core), blk: 4 (over x).
Axes of the slice: x: 4, y: 4, z: 8, core: 2. Of those that a mesh axis runs over, the one named last changes fastest.
Arguments:
- emissive: bfloat16 [512, 3072, 128], P('mode', 'blk'), may hold values from 0.099609375 to 3
- classes: int32 [3072], P('blk'), may hold values from 0 to 7
- emissivity: float32 [8, 8], replicated, may hold values from 0.1 to 0.9
- mode_ids: int32 [64], replicated, may hold values from 0 to 256, as said below
- view_factor: bfloat16 [64, 2, 3072, 3072], P('mode', None, 'blk'), may hold values from -0.3125 to 0.3125
Outputs:
- radiosity: bfloat16 [512, 3072, 128], P('mode', 'blk')
Inputs may be any that keep to these rules, and one draw needn't show every extreme that they name: `mode_ids`: 64 different azimuthal mode numbers; 0 and 256 are always among them.
All inputs are finite; a program needn't handle non-finite values.
Results may differ from a plain program's by a relative error of at most 0.008.
Values may be sent and summed in bfloat16 or wider, within the bound.
A program may use at most 64 MiB of HBM per device.

v0:
```python
import math

import jax
import jax.numpy as jnp
from jax import lax
from jax.sharding import PartitionSpec as P

A = 512


def tables(mode_ids):
    mode_count = mode_ids.shape[0]
    stations = jnp.arange(A, dtype=jnp.int32)
    twists = mode_ids[:, None] * stations[None, :] % A
    phases = twists.astype(jnp.float32) * (2.0 * math.pi / A)
    cosine = jnp.cos(phases)
    sine_part = jnp.sin(phases)
    forward = (
        jnp.stack([cosine, -sine_part], axis=1).reshape(2 * mode_count, A).astype(jnp.bfloat16)
    )
    real_only = (mode_ids == 0) | (mode_ids == A // 2)
    weight = jnp.where(real_only, 1.0 / A, 2.0 / A).astype(jnp.float32)[:, None]
    inverse = (
        jnp.stack([weight * cosine, -weight * sine_part], axis=1)
        .reshape(2 * mode_count, A)
        .astype(jnp.bfloat16)
    )
    return (forward, inverse)


def local(emissive, classes, emissivity, mode_ids, view_factor):
    columns = emissive.shape[2]
    class_count = emissivity.shape[0]
    band_count = emissivity.shape[1]
    mode_count = mode_ids.shape[0]
    onehot = (classes[:, None] == jnp.arange(class_count, dtype=jnp.int32)[None, :]).astype(
        jnp.float32
    )
    per_band = jnp.dot(onehot, emissivity, precision=lax.Precision.HIGHEST)
    emission = jnp.tile(per_band, (1, columns // band_count))
    emitted = (emission[None] * emissive.astype(jnp.float32)).astype(jnp.bfloat16)
    forward, inverse = tables(mode_ids)
    real_block = view_factor[0, 0]
    imag_block = view_factor[0, 1]
    slab_in = lax.all_to_all(emitted, "mode", split_axis=1, concat_axis=0, tiled=True)
    local_rows = slab_in.shape[1]
    item_count = slab_in.shape[2]
    spectrum = jnp.dot(
        forward, slab_in.reshape(A, local_rows * item_count), preferred_element_type=jnp.float32
    )
    spectrum = spectrum.astype(jnp.bfloat16).reshape(2 * mode_count, local_rows, item_count)
    modal_rows = lax.all_to_all(spectrum, "mode", split_axis=0, concat_axis=1, tiled=True)
    portion = lax.all_gather(modal_rows, "blk", axis=1, tiled=True)
    real_part = jnp.dot(real_block, portion[0], preferred_element_type=jnp.float32) - jnp.dot(
        imag_block, portion[1], preferred_element_type=jnp.float32
    )
    imag_part = jnp.dot(real_block, portion[1], preferred_element_type=jnp.float32) + jnp.dot(
        imag_block, portion[0], preferred_element_type=jnp.float32
    )
    reflected = jnp.stack([real_part, imag_part])
    reflected = reflected.astype(jnp.bfloat16)
    slab_in = lax.all_to_all(reflected, "mode", split_axis=1, concat_axis=0, tiled=True)
    local_rows = slab_in.shape[1]
    item_count = slab_in.shape[2]
    flattened = slab_in.reshape(2 * mode_count, local_rows * item_count)
    irradiance = jnp.dot(inverse.T, flattened, preferred_element_type=jnp.float32)
    irradiance = irradiance.astype(jnp.bfloat16).reshape(A, local_rows, item_count)
    irradiance = lax.all_to_all(irradiance, "mode", split_axis=0, concat_axis=1, tiled=True)
    radiosity = emitted.astype(jnp.float32) + (1.0 - emission)[None] * irradiance.astype(
        jnp.float32
    )
    return radiosity.astype(jnp.bfloat16)


def solution(mesh):
    placed = (P("mode", "blk", None), P("blk"), P(), P(), P("mode", None, "blk", None))
    return jax.shard_map(
        local, mesh=mesh, in_specs=placed, out_specs=P("mode", "blk", None), check_vma=False
    )
```

profile of v0, /device:TPU:1, one launch (start us, length us, event | category | flops | bytes accessed | tf_op | source)
XLA Modules:
  0.0 234.3 jit_solution(6293051335725933476)
XLA Ops:
  6.5 0.7 copy-done
  7.2 1.1 fusion.34
  8.3 0.6 copy-done.2
  8.9 0.2 copy.62
  9.1 3.8 %multiply_convert_fusion = bf16[8,768,128]{2,0,1:T(8,128)(2,1)} fusion(bf16[8,768,128]{2,1,0:T(8,128)(2,1)} %param.5, f32[768,128]{1,0:T(8,128)S(1)} %copy.62), kind=kLoop, calls=%fused_computation.16 | loop fusion | flops 2359296 | bytes 3538944 | tf_op jit(solution)/shard_map/convert_element_type | solution.py:41
  12.9 13.3 %all-to-all-start = ((bf16[8,768,128]{2,0,1:T(8,128)(2,1)}), bf16[8,768,128]{2,0,1:T(8,128)(2,1)S(1)}, u32[]{:S(2)}, u32[]{:S(2)}) async-start(bf16[8,768,128]{2,0,1:T(8,128)(2,1)} %multiply_convert_fusion), calls=%async_computation | async-start | bytes 3145728 | tf_op jit(solution)/shard_map/all_to_all | solution.py:45
  26.3 0.6 fusion.44
  27.1 38.1 %all-to-all-done = bf16[8,768,128]{2,0,1:T(8,128)(2,1)S(1)} async-done(((bf16[8,768,128]{2,0,1:T(8,128)(2,1)}), bf16[8,768,128]{2,0,1:T(8,128)(2,1)S(1)}, u32[]{:S(2)}, u32[]{:S(2)}) %all-to-all-start) | async-done | bytes 1572896 | tf_op jit(solution)/shard_map/all_to_all | solution.py:45
  65.2 0.4 convolution_convert_fusion.1
  65.6 0.2 copy.67
  65.8 0.4 copy.68
  66.2 24.0 %all_to_all.57 = bf16[128,12,128]{2,1,0:T(8,128)(2,1)S(1)} all-to-all(bf16[128,12,128]{2,1,0:T(8,128)(2,1)S(1)} %copy.68), channel_id=1, replica_groups=mesh['mode'=64,'blk'=4] {'mode'}, dimensions={0} | all-to-all | bytes 786432 | tf_op jit(solution)/shard_map/all_to_all | solution.py:52
  90.3 1.0 copy.70
  91.4 25.6 %all-gather.2.cloned.1.call-done = bf16[2,3072,128]{2,0,1:T(2,128)(2,1)} async-done(((bf16[2,768,128]{2,0,1:T(2,128)(2,1)}), bf16[2,3072,128]{2,0,1:T(2,128)(2,1)}) %all-gather.2.cloned.1.call-update) | async-done | bytes 1572880 | tf_op jit(solution)/shard_map/all_gather | solution.py:53
  116.9 4.6 %fusion.46 = (bf16[1,3072,128]{2,0,1:T(2,128)(2,1)S(1)}, bf16[1,3072,128]{2,0,1:T(2,128)(2,1)S(1)}) fusion(bf16[2,3072,128]{2,0,1:T(2,128)(2,1)} %all-gather.2.cloned.1.call-done), kind=kLoop, calls=%fused_computation.54 | loop fusion | bytes 3145728 | tf_op jit(solution)/shard_map/slice | solution.py:55
  121.6 4.2 %fusion.2 = f32[128,768]{1,0:T(8,128)S(1)} fusion(bf16[1,2,768,3072]{3,2,1,0:T(8,128)(2,1)} %param.9, bf16[1,3072,128]{2,0,1:T(2,128)(2,1)S(1)} %get-tuple-element.7), kind=kOutput, calls=%fused_computation.2 | convolution fusion | flops 603979776 | bytes 5898240 | tf_op jit(solution)/shard_map/dot_general | solution.py:54
  125.8 4.2 %fusion = f32[128,768]{1,0:T(8,128)S(1)} fusion(bf16[1,2,768,3072]{3,2,1,0:T(8,128)(2,1)} %param.9, bf16[1,3072,128]{2,0,1:T(2,128)(2,1)S(1)} %get-tuple-element.8), kind=kOutput, calls=%fused_computation | convolution fusion | flops 603979776 | bytes 5898240 | tf_op jit(solution)/shard_map/dot_general | solution.py:57
  130.1 4.2 %fusion.26 = bf16[1,768,128]{1,2,0:T(8,128)(2,1)S(1)} fusion(f32[128,768]{1,0:T(8,128)S(1)} %fusion.2, bf16[1,2,768,3072]{3,2,1,0:T(8,128)(2,1)} %param.9, bf16[1,3072,128]{2,0,1:T(2,128)(2,1)S(1)} %get-tuple-element.8), kind=kOutput, calls=%fused_computation.23 | convolution fusion | flops 604176384 | bytes 6094848 | tf_op jit(solution)/shard_map/dot_general | solution.py:54
  134.3 1.7 fusion.29
  136.0 1.1 copy.73
  137.1 10.9 %all-to-all-start.2 = ((bf16[2,768,128]{2,0,1:T(2,128)(2,1)}), bf16[2,768,128]{2,0,1:T(2,128)(2,1)S(1)}, u32[]{:S(2)}, u32[]{:S(2)}) async-start(bf16[2,768,128]{2,0,1:T(2,128)(2,1)} %copy.73), calls=%async_computation.2 | async-start | bytes 786432 | tf_op jit(solution)/shard_map/all_to_all | solution.py:62
  148.2 14.9 %all-to-all-done.2 = bf16[2,768,128]{2,0,1:T(2,128)(2,1)S(1)} async-done(((bf16[2,768,128]{2,0,1:T(2,128)(2,1)}), bf16[2,768,128]{2,0,1:T(2,128)(2,1)S(1)}, u32[]{:S(2)}, u32[]{:S(2)}) %all-to-all-start.2) | async-done | bytes 393248 | tf_op jit(solution)/shard_map/all_to_all | solution.py:62
  163.1 0.6 convolution_convert_fusion
  163.7 0.7 copy.75
  164.4 3.0 %copy.76 = bf16[512,12,128]{2,1,0:T(8,128)(2,1)} copy(bf16[512,12,128]{0,2,1:T(8,128)(2,1)S(1)} %bitcast.76) | data formatting | bytes 3145728 | tf_op jit(solution)/shard_map/reshape | solution.py:67
  167.5 5.7 %all-to-all-start.3 = ((bf16[512,12,128]{2,1,0:T(8,128)(2,1)}), bf16[512,12,128]{2,1,0:T(8,128)(2,1)S(1)}, u32[]{:S(2)}, u32[]{:S(2)}) async-start(bf16[512,12,128]{2,1,0:T(8,128)(2,1)} %copy.76), calls=%async_computation.3 | async-start | bytes 4194304 | tf_op jit(solution)/shard_map/all_to_all | solution.py:68
  173.4 49.5 %all-to-all-done.3 = bf16[512,12,128]{2,1,0:T(8,128)(2,1)S(1)} async-done(((bf16[512,12,128]{2,1,0:T(8,128)(2,1)}), bf16[512,12,128]{2,1,0:T(8,128)(2,1)S(1)}, u32[]{:S(2)}, u32[]{:S(2)}) %all-to-all-start.3) | async-done | bytes 1572896 | tf_op jit(solution)/shard_map/all_to_all | solution.py:68
  222.9 0.3 convert_bitcast_fusion
  223.2 0.4 copy.78
  223.6 1.0 copy-done.1
  224.6 1.5 fusion.13
  226.1 1.4 copy.79
  (28 shorter events, 0.9 us)
Async XLA Ops:
  6.5 0.7 copy-start
  8.3 0.6 copy-start.2
  12.9 13.3 %copy-start.4 = (s32[64]{0:T(128)S(1)}, s32[64]{0:T(128)}, u32[]{:S(2)}) copy-start(s32[64]{0:T(128)} %param.8) | copy-start | bytes 772
  12.9 52.3 %all-to-all-start = ((bf16[8,768,128]{2,0,1:T(8,128)(2,1)}), bf16[8,768,128]{2,0,1:T(8,128)(2,1)S(1)}, u32[]{:S(2)}, u32[]{:S(2)}) async-start(bf16[8,768,128]{2,0,1:T(8,128)(2,1)} %multiply_convert_fusion), calls=%async_computation | async-start | bytes 3145728 | tf_op jit(solution)/shard_map/all_to_all | solution.py:45
  26.2 90.8 %all-gather.2.cloned.1.call-start = ((), (), s32[]{:S(2)}) async-start(), calls=%async_computation.4 | async-start | bytes 1966080 | tf_op jit(solution)/shard_map/all_gather | solution.py:53
  121.6 12.7 %slice-start = ((s8[9437184]{0:T(1024)(128)(4,1)}), s8[4194304]{0:T(1024)(128)(4,1)S(1)}, s32[]{:S(2)}) async-start(s8[9437184]{0:T(1024)(128)(4,1)} %bitcast.82), calls=%async_computation.5 | async-start | bytes 8388608
  125.8 8.4 %slice-start.1 = ((s8[9437184]{0:T(1024)(128)(4,1)}), s8[4194304]{0:T(1024)(128)(4,1)S(1)}, s32[]{:S(2)}) async-start(s8[9437184]{0:T(1024)(128)(4,1)} %bitcast.82), calls=%async_computation.6 | async-start | bytes 8388608
  130.1 4.2 %slice-start.2 = ((s8[9437184]{0:T(1024)(128)(4,1)}), s8[1048576]{0:T(1024)(128)(4,1)S(1)}, s32[]{:S(2)}) async-start(s8[9437184]{0:T(1024)(128)(4,1)} %bitcast.82), calls=%async_computation.7 | async-start | bytes 2097152
  137.1 25.9 %all-to-all-start.2 = ((bf16[2,768,128]{2,0,1:T(2,128)(2,1)}), bf16[2,768,128]{2,0,1:T(2,128)(2,1)S(1)}, u32[]{:S(2)}, u32[]{:S(2)}) async-start(bf16[2,768,128]{2,0,1:T(2,128)(2,1)} %copy.73), calls=%async_computation.2 | async-start | bytes 786432 | tf_op jit(solution)/shard_map/all_to_all | solution.py:62
  167.5 5.7 %copy-start.3 = (f32[768,8]{0,1:T(8,128)S(1)}, f32[768,8]{0,1:T(8,128)}, u32[]{:S(2)}) copy-start(f32[768,8]{0,1:T(8,128)} %copy-done.2) | copy-start | bytes 73732
  167.5 55.4 %all-to-all-start.3 = ((bf16[512,12,128]{2,1,0:T(8,128)(2,1)}), bf16[512,12,128]{2,1,0:T(8,128)(2,1)S(1)}, u32[]{:S(2)}, u32[]{:S(2)}) async-start(bf16[512,12,128]{2,1,0:T(8,128)(2,1)} %copy.76), calls=%async_computation.3 | async-start | bytes 4194304 | tf_op jit(solution)/shard_map/all_to_all | solution.py:68
  223.2 1.4 copy-start.1
Sparse Core Ops, SparseCore 0:
  91.5 25.4 all-gather.1
where the time goes:
time: 235 us; the launch traced here: 234 us
  waiting for transfers between devices  128 us (54%)
  starting transfers between devices  29.9 us (13%)
  blocking collectives  24 us (10%)
  matrix products  16.3 us (7%)
  local copies, waits for them, and re-layouts  16.2 us (7%)
  between operations  13.7 us (6%)
  other arithmetic  6.3 us (3%)
    all_to_all x1, waiting for transfers between devices, local(): lax.all_to_all(irradiance, 'mode', split_axis=0, concat_axis=1, tiled=True)  49.5 us
    all_to_all x1, waiting for transfers between devices, local(): lax.all_to_all(emitted, 'mode', split_axis=1, concat_axis=0, tiled=True)  38.1 us
    all_gather x1, waiting for transfers between devices, local(): portion = lax.all_gather(modal_rows, 'blk', axis=1, tiled=True)  25.6 us
    all_to_all x1, blocking collectives, local(): lax.all_to_all(spectrum, 'mode', split_axis=0, concat_axis=1, tiled=True)  24 us
    all_to_all x1, waiting for transfers between devices, local(): lax.all_to_all(reflected, 'mode', split_axis=1, concat_axis=0, tiled=True)  14.9 us
    all_to_all x1, starting transfers between devices, local(): lax.all_to_all(emitted, 'mode', split_axis=1, concat_axis=0, tiled=True)  13.3 us
    all_to_all x1, starting transfers between devices, local(): lax.all_to_all(reflected, 'mode', split_axis=1, concat_axis=0, tiled=True)  10.9 us
    all_to_all x1, starting transfers between devices, local(): lax.all_to_all(irradiance, 'mode', split_axis=0, concat_axis=1, tiled=True)  5.72 us
  transfers between devices with their start and end apart: 4, of which 4 were waited for; matrix products, arithmetic and copies ran while one was open for 1% of the time, Pallas kernels for 0%

commit v1 on v0

v1 whole, which is shorter than its diff:
```python
import functools
import math

import jax
import jax.numpy as jnp
from jax import lax
from jax.experimental import pallas as pl
from jax.experimental.pallas import tpu as pltpu
from jax.sharding import PartitionSpec as P

A = 512
Z, Y, CORES, X = 8, 4, 2, 4
Q = Y * CORES
S = A // (Z * Q)
SZ = S * Q
T = 16
NC = 3
PATCHES = 768
PC = PATCHES // NC
W = PC // Q
G = W // T
C = 128
R = 2 * Q
RT = R * T
MESH = pl.DeviceIdType.MESH
F32, BF16 = jnp.float32, jnp.bfloat16


def tables(mode_ids, stations):
    twists = mode_ids[:, None] * stations[None, :] % A
    phases = twists.astype(F32) * (2.0 * math.pi / A)
    cosine, sine = jnp.cos(phases), jnp.sin(phases)
    rows = 2 * mode_ids.shape[0]
    forward = jnp.stack([cosine, -sine], axis=1).reshape(rows, -1)
    real_only = (mode_ids == 0) | (mode_ids == A // 2)
    weight = jnp.where(real_only, 1.0 / A, 2.0 / A).astype(F32)[:, None]
    inverse = jnp.stack([weight * cosine, -weight * sine], axis=1).reshape(rows, -1)
    return forward, inverse


def spread(table_ref, out_ref):
    rows, width = table_ref.shape
    mask = lax.broadcasted_iota(jnp.int32, (T, width), 0) == (
        lax.broadcasted_iota(jnp.int32, (T, width), 1) % T
    )

    def body(b, _):
        block = table_ref[pl.ds(pl.multiple_of(b * 8, 8), 8), :]
        for i in range(8):
            row = jnp.broadcast_to(block[i : i + 1, :], (T, width))
            at = pl.multiple_of((b * 8 + i) * T, T)
            out_ref[pl.ds(at, T), :] = jnp.where(mask, row, 0.0).astype(BF16)
        return 0

    lax.fori_loop(0, rows // 8, body, 0)


def kernel(
    emissive, emission, ftab, itab, factor_hbm, out,
    fk, ik, factor, emitted, station, rs_out, rs_in, spec, xs, acc, refl, gath, irr_out, irr,
    f_sem, a_send, a_recv, rs_send, rs_recv, c_send, c_recv, x_send, x_recv,
    d_send, d_recv, g_send, g_recv, h_send, h_recv,
):
    me, x = lax.axis_index("mode"), lax.axis_index("blk")
    z, q = me // Q, me % Q
    y, core = q // CORES, q % CORES

    def at_q(other):
        return {"mode": z * Q + other, "blk": x}

    def at_z(step):
        return {"mode": ((z + step + Z) % Z) * Q + q, "blk": x}

    def at_x(step):
        return {"mode": me, "blk": (x + step + X) % X}

    def copy(src, dst, send, recv, device):
        return pltpu.make_async_remote_copy(
            src_ref=src, dst_ref=dst, send_sem=send, recv_sem=recv,
            device_id=device, device_id_type=MESH,
        )

    sent = []

    def send(src, dst, s, r, device):
        op = copy(src, dst, s, r, device)
        op.start()
        sent.append(op)

    def arrived(dst, s, r):
        copy(dst, dst, s, r, at_z(1)).wait_recv()

    load = pltpu.make_async_copy(factor_hbm, factor, f_sem)
    load.start()

    barrier = pltpu.get_barrier_semaphore()
    peers = [at_q((q + k) % Q) for k in range(1, Q)]
    peers += [at_z(1), at_z(-1), at_x(1), at_x(-1)]
    for device in peers:
        pl.semaphore_signal(barrier, inc=1, device_id=device, device_id_type=MESH)

    def rows_of(c, other):
        return pl.ds(pl.multiple_of(c * PC + other * W, T), W)

    def emit(c):
        rows = pl.ds(c * PC, PC)
        share = emission[rows, :]

        def body(s, _):
            emitted[s, rows, :] = (share * emissive[s, rows, :].astype(F32)).astype(BF16)
            return 0

        lax.fori_loop(0, S, body, 0)

    def stations_out(c):
        for k in range(1, Q):
            other = (q + k) % Q
            send(
                emitted.at[:, rows_of(c, other), :], station.at[c, pl.ds(q * S, S)],
                a_send.at[c, k], a_recv.at[c, k], at_q(other),
            )
        station[c, pl.ds(q * S, S)] = emitted[:, rows_of(c, q), :]

    def stations_in(c):
        for k in range(1, Q):
            other = (q - k + Q) % Q
            arrived(station.at[c, pl.ds(other * S, S)], a_send.at[c, k], a_recv.at[c, k])

    def partial(c, target):
        parts = [station[c, :, g * T : (g + 1) * T, :].reshape(SZ * T, C) for g in range(G)]
        right = parts[0] if G == 1 else jnp.concatenate(parts, axis=1)
        left = fk[pl.ds(pl.multiple_of(target * RT, RT), RT), :]
        return jnp.dot(left, right, preferred_element_type=F32)

    def piece(value, g):
        return value[:, g * C : (g + 1) * C].reshape(R, T, C)

    def rs_step(c, t):
        half = R // 2
        if t == 0:
            stations_in(c)
            value = partial(c, (z + 4) % Z)
            for way in range(2):
                rows = slice(way * half, (way + 1) * half)
                for g in range(G):
                    rs_out[way, c, 0, rows, g * T : (g + 1) * T, :] = piece(value, g)[rows].astype(BF16)
                where = pl.ds(way * half, half)
                send(
                    rs_out.at[way, c, 0, where], rs_in.at[way, c, 0, where],
                    rs_send.at[way, c, 0], rs_recv.at[way, c, 0], at_z(1 - 2 * way),
                )
            return
        for way in range(2):
            target = (z + 4 - t) % Z if way == 0 else (z + 4 + t) % Z
            value = partial(c, target)
            if t == 1:
                where = pl.ds(way * half, half)
                arrived(rs_in.at[way, c, 0, where], rs_send.at[way, c, 0], rs_recv.at[way, c, 0])
            else:
                arrived(rs_in.at[way, c, t - 1], rs_send.at[way, c, t - 1], rs_recv.at[way, c, t - 1])
            for g in range(G):
                cols = slice(g * T, (g + 1) * T)
                mine = piece(value, g)
                if t == 1:
                    hit = slice(way * half, (way + 1) * half)
                    miss = slice((1 - way) * half, (2 - way) * half)
                    total = mine[hit] + rs_in[way, c, 0, hit, cols, :].astype(F32)
                    rs_out[way, c, t, hit, cols, :] = total.astype(BF16)
                    rs_out[way, c, t, miss, cols, :] = mine[miss].astype(BF16)
                else:
                    total = mine + rs_in[way, c, t - 1, :, cols, :].astype(F32)
                    rs_out[way, c, t, :, cols, :] = total.astype(BF16)
            send(
                rs_out.at[way, c, t], rs_in.at[way, c, t],
                rs_send.at[way, c, t], rs_recv.at[way, c, t], at_z(1 - 2 * way),
            )

    def rs_final(c):
        value = partial(c, z)
        for way in range(2):
            arrived(rs_in.at[way, c, 3], rs_send.at[way, c, 3], rs_recv.at[way, c, 3])
        for g in range(G):
            cols = slice(g * T, (g + 1) * T)
            total = piece(value, g) + (
                rs_in[0, c, 3, :, cols, :].astype(F32) + rs_in[1, c, 3, :, cols, :].astype(F32)
            )
            spec[c, :, cols, :] = total.astype(BF16)
        for k in range(1, Q):
            other = (q + k) % Q
            send(
                spec.at[c, pl.ds(other * 2, 2)], xs.at[x, :, rows_of(c, q), :],
                c_send.at[c, k], c_recv.at[c, k], at_q(other),
            )
        xs[x, :, rows_of(c, q), :] = spec[c, pl.ds(q * 2, 2)]

    def gather_first(c):
        for k in range(1, Q):
            other = (q - k + Q) % Q
            arrived(xs.at[x, :, rows_of(c, other), :], c_send.at[c, k], c_recv.at[c, k])
        rows = pl.ds(c * PC, PC)
        for way in range(2):
            send(
                xs.at[x, :, rows, :], xs.at[x, :, rows, :],
                x_send.at[0, way, c], x_recv.at[0, way, c], at_x(1 - 2 * way),
            )

    def reflect(c, source):
        rows = pl.ds(c * PC, PC)
        real, imag = xs[source, 0, rows, :], xs[source, 1, rows, :]
        right = jnp.concatenate(
            [jnp.concatenate([real, imag], axis=1), jnp.concatenate([-imag, real], axis=1)], axis=0
        )
        at = pl.ds(pl.multiple_of(source * PATCHES + c * PC, PC), PC)

        def body(b, _):
            to = pl.ds(pl.multiple_of(b * 256, 256), 256)
            left = jnp.concatenate([factor[0, to, at], factor[1, to, at]], axis=1)
            acc[to, :] += jnp.dot(left, right, preferred_element_type=F32)
            return 0

        lax.fori_loop(0, PATCHES // 256, body, 0)

    def gather_second(c):
        rows = pl.ds(c * PC, PC)
        reflect(c, x)
        for way in range(2):
            source = (x + X - 1 + 2 * way) % X
            arrived(xs.at[source, :, rows, :], x_send.at[0, way, c], x_recv.at[0, way, c])
            send(
                xs.at[source, way, rows, :], xs.at[source, way, rows, :],
                x_send.at[1, way, c], x_recv.at[1, way, c], at_x(1 - 2 * way),
            )
        for way in range(2):
            reflect(c, (x + X - 1 + 2 * way) % X)

    def gather_third(c):
        rows = pl.ds(c * PC, PC)
        source = (x + 2) % X
        for way in range(2):
            arrived(xs.at[source, way, rows, :], x_send.at[1, way, c], x_recv.at[1, way, c])
        reflect(c, source)

    def reflected_out(c):
        rows = pl.ds(c * PC, PC)
        for part in range(2):
            refl[part, rows, :] = acc[rows, part * C : (part + 1) * C].astype(BF16)
        for k in range(1, Q):
            other = (q + k) % Q
            send(
                refl.at[:, rows_of(c, other), :], gath.at[c, z, pl.ds(q * 2, 2)],
                d_send.at[c, k], d_recv.at[c, k], at_q(other),
            )
        gath[c, z, pl.ds(q * 2, 2)] = refl[:, rows_of(c, q), :]

    def ag_step(c, t):
        half = R // 2
        if t == 0:
            for k in range(1, Q):
                other = (q - k + Q) % Q
                arrived(gath.at[c, z, pl.ds(other * 2, 2)], d_send.at[c, k], d_recv.at[c, k])
        for way in range(2):
            source = (z - t + Z) % Z if way == 0 else (z + t) % Z
            if t > 0:
                arrived(gath.at[c, source], g_send.at[way, c, t - 1], g_recv.at[way, c, t - 1])
            block = gath.at[c, source]
            if t == 3:
                block = gath.at[c, source, pl.ds(way * half, half)]
            send(block, block, g_send.at[way, c, t], g_recv.at[way, c, t], at_z(1 - 2 * way))

    def irradiance_out(c):
        half = R // 2
        far = (z + 4) % Z
        for way in range(2):
            arrived(
                gath.at[c, far, pl.ds(way * half, half)], g_send.at[way, c, 3], g_recv.at[way, c, 3]
            )
        parts = [gath[c, :, :, g * T : (g + 1) * T, :].reshape(Z * RT, C) for g in range(G)]
        right = parts[0] if G == 1 else jnp.concatenate(parts, axis=1)
        rows = 2 * S * T
        for k in range(Y):
            other = (y + k) % Y
            left = ik[pl.ds(pl.multiple_of(other * rows, rows), rows), :]
            value = jnp.dot(left, right, preferred_element_type=F32)
            for g in range(G):
                irr_out[c, pl.ds(other * 2 * S, 2 * S), g * T : (g + 1) * T, :] = (
                    value[:, g * C : (g + 1) * C].reshape(2 * S, T, C).astype(BF16)
                )
            for j in range(CORES):
                if k == 0 and j == 0:
                    continue
                to = other * CORES + (core + j) % CORES
                n = k * CORES + j
                send(
                    irr_out.at[c, pl.ds(to * S, S)], irr.at[:, rows_of(c, q), :],
                    h_send.at[c, n], h_recv.at[c, n], at_q(to),
                )
        irr[:, rows_of(c, q), :] = irr_out[c, pl.ds(q * S, S)]

    def finish(c):
        for k in range(Y):
            for j in range(CORES):
                if k == 0 and j == 0:
                    continue
                source = ((y - k + Y) % Y) * CORES + (core + j) % CORES
                n = k * CORES + j
                arrived(irr.at[:, rows_of(c, source), :], h_send.at[c, n], h_recv.at[c, n])
        rows = pl.ds(c * PC, PC)
        rest = 1.0 - emission[rows, :]

        def body(s, _):
            total = emitted[s, rows, :].astype(F32) + rest * irr[s, rows, :].astype(F32)
            out[s, rows, :] = total.astype(BF16)
            return 0

        lax.fori_loop(0, S, body, 0)

    emit(0)
    pl.semaphore_wait(barrier, len(peers))
    stations_out(0)
    for c in range(1, NC):
        emit(c)
        stations_out(c)
    spread(ftab, fk)
    spread(itab, ik)
    acc[...] = jnp.zeros_like(acc)

    stages = [functools.partial(rs_step, t=t) for t in range(4)]
    stages += [rs_final, gather_first, gather_second, gather_third]
    loaded = False
    for slot in range(len(stages) + NC - 1):
        for c in range(NC):
            stage = slot - c
            if 0 <= stage < len(stages):
                if stages[stage] is gather_second and not loaded:
                    load.wait()
                    loaded = True
                stages[stage](c)
    for c in range(NC):
        reflected_out(c)
    for t in range(4):
        for c in range(NC):
            ag_step(c, t)
    for c in range(NC):
        irradiance_out(c)
    for c in range(NC):
        finish(c)
    for op in sent:
        op.wait_send()


def local(emissive, classes, emissivity, mode_ids, view_factor):
    pick = classes[:, None] == jnp.arange(emissivity.shape[0], dtype=jnp.int32)[None, :]
    rates = jnp.tile(emissivity, (1, C // emissivity.shape[1]))
    emission = jnp.sum(jnp.where(pick[:, :, None], rates[None], 0.0), axis=1)
    z = lax.axis_index("mode") // Q
    forward, inverse = tables(mode_ids, z * SZ + jnp.arange(SZ, dtype=jnp.int32))
    ftab = jnp.repeat(forward, T, axis=1)
    itab = jnp.repeat(inverse.T, T, axis=1)
    vmem = pl.BlockSpec(memory_space=pltpu.VMEM)
    dma = pltpu.SemaphoreType.DMA
    return pl.pallas_call(
        kernel,
        out_shape=jax.ShapeDtypeStruct(emissive.shape, BF16),
        in_specs=[vmem] * 4 + [pl.BlockSpec(memory_space=pl.ANY)],
        out_specs=vmem,
        scratch_shapes=[
            pltpu.VMEM((Z * RT, SZ * T), BF16),
            pltpu.VMEM((SZ * T, Z * RT), BF16),
            pltpu.VMEM((2, PATCHES, X * PATCHES), BF16),
            pltpu.VMEM((S, PATCHES, C), BF16),
            pltpu.VMEM((NC, SZ, W, C), BF16),
            pltpu.VMEM((2, NC, 4, R, W, C), BF16),
            pltpu.VMEM((2, NC, 4, R, W, C), BF16),
            pltpu.VMEM((NC, R, W, C), BF16),
            pltpu.VMEM((X, 2, PATCHES, C), BF16),
            pltpu.VMEM((PATCHES, 2 * C), F32),
            pltpu.VMEM((2, PATCHES, C), BF16),
            pltpu.VMEM((NC, Z, R, W, C), BF16),
            pltpu.VMEM((NC, SZ, W, C), BF16),
            pltpu.VMEM((S, PATCHES, C), BF16),
            dma,
            dma((NC, Q)), dma((NC, Q)),
            dma((2, NC, 4)), dma((2, NC, 4)),
            dma((NC, Q)), dma((NC, Q)),
            dma((2, 2, NC)), dma((2, 2, NC)),
            dma((NC, Q)), dma((NC, Q)),
            dma((2, NC, 4)), dma((2, NC, 4)),
            dma((NC, Q)), dma((NC, Q)),
        ],
        compiler_params=pltpu.CompilerParams(
            collective_id=0, has_side_effects=True, vmem_limit_bytes=56 * 2**20
        ),
    )(emissive, emission, ftab, itab, view_factor[0])


def solution(mesh):
    placed = (P("mode", "blk", None), P("blk"), P(), P(), P("mode", None, "blk", None))
    return jax.shard_map(
        local, mesh=mesh, in_specs=placed, out_specs=P("mode", "blk", None), check_vma=False
    )
```

time: 235 us -> 141 us (0.60)
  Pallas kernels: 0 us -> 128 us
  waiting for transfers between devices: 128 us -> 0 us
  starting transfers between devices: 29.9 us -> 0 us
  blocking collectives: 24 us -> 0 us
  matrix products: 16.3 us -> 0 us
  between operations: 13.7 us -> 0.06 us
  local copies, waits for them, and re-layouts: 16.2 us -> 5.86 us
    pallas_call x0 -> x1, Pallas kernels: none -> 128 us  [local(): pl.pallas_call(kernel, out_shape=jax.ShapeDtypeStruct(emissive.shape, BF1...]
    all_to_all x3 -> x0, waiting for transfers between devices: 102 us -> none  [the longest x1 49.5 us: local(): lax.all_to_all(irradiance, 'mode', split_axis=0, concat_axis=1, tiled=True)]
    all_to_all x3 -> x0, starting transfers between devices: 29.9 us -> none  [the longest x1 13.3 us: local(): lax.all_to_all(emitted, 'mode', split_axis=1, concat_axis=0, tiled=True)]
    all_gather x1 -> x0, waiting for transfers between devices: 25.6 us -> none  [local(): portion = lax.all_gather(modal_rows, 'blk', axis=1, tiled=True)]
    all_to_all x1 -> x0, blocking collectives: 24 us -> none  [local(): lax.all_to_all(spectrum, 'mode', split_axis=0, concat_axis=1, tiled=True)]
    dot_general x7 -> x0, matrix products: 16.3 us -> none  [the longest x1 4.22 us: local(): jnp.dot(imag_block, portion[0], preferred_element_type=jnp.float32)]
    convert_element_type x3 -> x0, other arithmetic: 5.58 us -> none  [the longest x1 3.79 us: local(): (emission[None] * emissive.astype(jnp.float32)).astype(jnp.bfloat16)]
    reduce_sum x0 -> x1, other arithmetic: none -> 4.97 us  [local(): emission = jnp.sum(jnp.where(pick[:, :, None], rates[None], 0.0), axis=1)]
  transfers between devices with their start and end apart: 4 -> 0, of which waited for: 4 -> 0; matrix products, arithmetic and copies ran while one was open for 1% -> 0% of each run, Pallas kernels for 0% -> 0%
where the time goes in v1:
time: 141 us
  Pallas kernels  128 us (91%)
  other arithmetic  7.37 us (5%)
  local copies, waits for them, and re-layouts  5.86 us (4%)
    pallas_call x1, Pallas kernels, local(): pl.pallas_call(kernel, out_shape=jax.ShapeDtypeStruct(emissive.shape, BF1...  128 us
    reduce_sum x1, other arithmetic, local(): emission = jnp.sum(jnp.where(pick[:, :, None], rates[None], 0.0), axis=1)  4.97 us

profile of v1, /device:TPU:1, one launch (start us, length us, event | category | flops | bytes accessed | tf_op | source)
XLA Modules:
  0.0 141.0 jit_solution(8900455242255392931)
XLA Ops:
  0.0 0.7 fusion.6
  0.7 0.7 tile.8
  1.4 0.1 tile.9
  1.4 0.9 iota_compare_fusion
  2.3 0.9 broadcast_multiply_fusion.1
  3.2 0.1 copy.16
  3.3 0.1 copy.17
  3.3 0.1 copy.18
  3.4 5.0 %select_reduce_fusion.emission = f32[768,128]{1,0:T(8,128)} fusion(f32[8,128]{1,0:T(8,128)S(1)} %tile.9, pred[768,8]{1,0:T(8,128)(4,1)S(1)} %iota_compare_fusion), kind=kLoop, calls=%fused_computation | loop fusion | flops 1474560 | bytes 403456 | tf_op jit(solution)/shard_map/reduce_sum | solution.py:354
  8.4 1.0 copy.19.ftab
  9.4 0.1 broadcast_in_dim.46
  9.5 1.1 copy.20.itab
  10.6 127.7 %shard_map.55 = bf16[8,768,128]{2,1,0:T(8,128)(2,1)} custom-call(bf16[8,768,128]{2,1,0:T(8,128)(2,1)} %emissive.1, f32[768,128]{1,0:T(8,128)} %select_reduce_fusion.emission, f32[128,1024]{1,0:T(8,128)} %copy.19.ftab, f32[64,2048]{1,0:T(8,128)} %copy.20.itab, bf16[2,768,3072]{2,1,0:T(8,128)(2,1)} %bitcast.7), custom_call_target="tpu_custom_call" | custom-call | tf_op jit(solution)/shard_map/pallas_call | solution.py:361
  138.3 2.7 %copy.22 = bf16[8,768,128]{2,1,0:T(8,128)(2,1)} copy(bf16[8,768,128]{2,1,0:T(8,128)(2,1)} %shard_map.55) | data formatting | bytes 3145728
  (3 shorter events, 0.1 us)

commit v2 on v1

v2 whole, which is shorter than its diff:
```python
import functools
import math

import jax
import jax.numpy as jnp
from jax import lax
from jax.experimental import pallas as pl
from jax.experimental.pallas import tpu as pltpu
from jax.sharding import PartitionSpec as P

A = 512
Z, Y, CORES, X = 8, 4, 2, 4
Q = Y * CORES
S = A // (Z * Q)
SZ = S * Q
T = 16
L = 64
HALVES = ((16, 32), (16, 16, 16))
CHUNKS = tuple((h, sum(ws[:n]), w) for h, ws in enumerate(HALVES) for n, w in enumerate(ws))
NC = len(CHUNKS)
FIRST = tuple(n for n, c in enumerate(CHUNKS) if c[1] == 0)
LAST = tuple(n - 1 for n in FIRST[1:] + (NC,))
W = sum(HALVES[0])
PAIRS = W * Q
PATCHES = 2 * PAIRS
C = 128
R = 2 * Q
RT = R * T
MODES = Z * Q
MESH = pl.DeviceIdType.MESH
F32, BF16 = jnp.float32, jnp.bfloat16
HIGHEST = lax.Precision.HIGHEST
ORDER = (
    0, 1, 0, 3, 4, 0, 1, 0, 1, 4, 0, 1, 2, 1, 0, 2, 4, 1, 3, 0, 2, 4, 0, 3, 1, 2, 4, 0, 3, 1,
    3, 1, 2, 3, 4, 0, 2, 1, 3, 4, 2, 0, 1, 3, 4, 2, 0, 3, 1, 2, 4, 0, 1, 2, 4, 3, 1, 2, 4, 3,
    0, 2, 4, 2, 4, 3, 2, 3, 4, 0, 3, 1, 2, 4, 3,
)


def iota(shape, axis):
    return lax.broadcasted_iota(jnp.int32, shape, axis)


def flag(where):
    return jnp.where(where, 1.0, 0.0)


def swap(value):
    return pltpu.roll(value, L, 1)


def pack(left, right):
    return jnp.where(iota(left.shape, 1) < L, left, right)


def spread(table_ref, out_ref):
    rows, width = table_ref.shape
    mask = iota((T, width), 0) == iota((T, width), 1) % T

    def body(b, _):
        block = table_ref[pl.ds(pl.multiple_of(b * 8, 8), 8), :]
        for i in range(8):
            row = jnp.broadcast_to(block[i : i + 1, :], (T, width))
            at = pl.multiple_of((b * 8 + i) * T, T)
            out_ref[pl.ds(at, T), :] = jnp.where(mask, row, 0.0).astype(BF16)
        return 0

    lax.fori_loop(0, rows // 8, body, 0)


def kernel(
    emissive, classes, emissivity, mode_ids, factor_hbm, out,
    emission, ftab, itab, fk, ik, factor, emitted, station, rs_out, rs_in, spec, xs, acc, refl,
    gath, irr_out, irr,
    f_sem, a_send, a_recv, rs_send, rs_recv, c_send, c_recv, x_send, x_recv,
    d_send, d_recv, g_send, g_recv, h_send, h_recv,
):
    me, x = lax.axis_index("mode"), lax.axis_index("blk")
    z, q = me // Q, me % Q
    y, core = q // CORES, q % CORES

    def at_q(other):
        return {"mode": z * Q + other, "blk": x}

    def at_z(step):
        return {"mode": ((z + step + Z) % Z) * Q + q, "blk": x}

    def at_x(step):
        return {"mode": me, "blk": (x + step + X) % X}

    def copy(src, dst, send, recv, device):
        return pltpu.make_async_remote_copy(
            src_ref=src, dst_ref=dst, send_sem=send, recv_sem=recv,
            device_id=device, device_id_type=MESH,
        )

    sent = []
    begun = []

    def send(src, dst, s, r, device):
        op = copy(src, dst, s, r, device)
        op.start()
        sent.append(op)

    def arrived(dst, s, r):
        copy(dst, dst, s, r, at_z(1)).wait_recv()

    load = pltpu.make_async_copy(factor_hbm, factor, f_sem)
    load.start()

    barrier = pltpu.get_barrier_semaphore()
    peers = [at_q((q + k) % Q) for k in range(1, Q)]
    peers += [at_z(1), at_z(-1), at_x(1), at_x(-1)]
    for device in peers:
        pl.semaphore_signal(barrier, inc=1, device_id=device, device_id_type=MESH)

    def cols(c):
        h, at, w = CHUNKS[c]
        return pl.ds(h * W + at, w)

    def rows(c, bottom=0):
        _, at, w = CHUNKS[c]
        return pl.ds(at * Q + bottom * PAIRS, w * Q)

    def rows_of(c, other):
        _, at, w = CHUNKS[c]
        return pl.ds(pl.multiple_of(at * Q + other * w, T), w)

    def tiles(c):
        h, at, w = CHUNKS[c]
        return [slice(h * W + at + t, h * W + at + t + T) for t in range(0, w, T)]

    def absorb():
        rates = jnp.dot(
            emissivity[...], flag(iota((Q, C), 1) % Q == iota((Q, C), 0)),
            precision=HIGHEST, preferred_element_type=F32,
        )
        pick = flag(iota((Q, PATCHES), 0) == jnp.broadcast_to(classes[...], (Q, PATCHES)))
        value = lax.dot_general(
            pick, rates, (((0,), (0,)), ((), ())), precision=HIGHEST, preferred_element_type=F32
        )
        emission[...] = pack(value[:PAIRS], value[PAIRS:])

    def transforms():
        ids = jnp.broadcast_to(mode_ids[...], (8, MODES)).astype(F32).astype(BF16)
        twin = flag(iota((MODES, 2 * MODES), 1) // 2 == iota((MODES, 2 * MODES), 0)).astype(BF16)
        ids = jnp.dot(ids, twin, preferred_element_type=F32)[0:1, :]
        shape = (SZ, 2 * MODES)
        stations = (iota(shape, 0) + z * SZ).astype(F32)
        quarter = (iota(shape, 1) % 2 * (A // 4)).astype(F32)
        twists = ids * stations + quarter
        twists = twists - A * jnp.floor(twists * (1.0 / A))
        waves = jnp.cos(twists * (2.0 * math.pi / A))
        weight = jnp.where((ids == 0) | (ids == A // 2), 1.0 / A, 2.0 / A)
        forward = waves.T.astype(BF16)
        inverse = (weight * waves).astype(BF16)
        repeat = flag(iota((SZ, SZ * T), 1) // T == iota((SZ, SZ * T), 0)).astype(BF16)
        ftab[...] = jnp.dot(forward, repeat, preferred_element_type=F32)
        repeat = flag(iota((Z * R, Z * RT), 1) // T == iota((Z * R, Z * RT), 0)).astype(BF16)
        itab[...] = jnp.dot(inverse, repeat, preferred_element_type=F32)
        spread(ftab, fk)
        spread(itab, ik)

    def emit(c):
        h = CHUNKS[c][0]
        share = emission[rows(c), :]

        def body(s, _):
            top = emissive[s, rows(c), :].astype(F32)
            bottom = emissive[s, rows(c, 1), :].astype(F32)
            value = pack(top, swap(bottom)) if h == 0 else pack(swap(top), bottom)
            emitted[h, s, rows(c), :] = (share * value).astype(BF16)
            return 0

        lax.fori_loop(0, S, body, 0)

    def stations_out(c):
        for k in range(1, Q):
            other = (q + k) % Q
            send(
                emitted.at[CHUNKS[c][0], :, rows_of(c, other), :], station.at[pl.ds(q * S, S), cols(c), :],
                a_send.at[c, k], a_recv.at[c, k], at_q(other),
            )
        station[pl.ds(q * S, S), cols(c), :] = emitted[CHUNKS[c][0], :, rows_of(c, q), :]

    def stations_in(c):
        for k in range(1, Q):
            other = (q - k + Q) % Q
            arrived(
                station.at[pl.ds(other * S, S), cols(c), :], a_send.at[c, k], a_recv.at[c, k]
            )

    def wide(parts):
        return parts[0] if len(parts) == 1 else jnp.concatenate(parts, axis=1)

    def partial(c, target):
        right = wide([station[:, t, :].reshape(SZ * T, C) for t in tiles(c)])
        left = fk[pl.ds(pl.multiple_of(target * RT, RT), RT), :]
        value = jnp.dot(left, right, preferred_element_type=F32)
        return [
            (t, value[:, g * C : (g + 1) * C].reshape(R, T, C)) for g, t in enumerate(tiles(c))
        ]

    half = R // 2

    def rs_step(c, t):
        if t == 0:
            stations_in(c)
            value = partial(c, (z + 4) % Z)
            for way in range(2):
                hit = slice(way * half, (way + 1) * half)
                for at, mine in value:
                    rs_out[way, 0, hit, at, :] = mine[hit].astype(BF16)
                block = (way, 0, pl.ds(way * half, half), cols(c))
                send(
                    rs_out.at[block], rs_in.at[block],
                    rs_send.at[way, c, 0], rs_recv.at[way, c, 0], at_z(1 - 2 * way),
                )
            return
        for way in range(2):
            value = partial(c, (z + 4 - t) % Z if way == 0 else (z + 4 + t) % Z)
            hit = slice(way * half, (way + 1) * half) if t == 1 else slice(0, R)
            miss = slice((1 - way) * half, (2 - way) * half)
            block = (way, t - 1, pl.ds(hit.start, hit.stop - hit.start), cols(c))
            arrived(rs_in.at[block], rs_send.at[way, c, t - 1], rs_recv.at[way, c, t - 1])
            for at, mine in value:
                total = mine[hit] + rs_in[way, t - 1, hit, at, :].astype(F32)
                rs_out[way, t, hit, at, :] = total.astype(BF16)
                if t == 1:
                    rs_out[way, t, miss, at, :] = mine[miss].astype(BF16)
            block = (way, t, slice(None), cols(c))
            send(
                rs_out.at[block], rs_in.at[block],
                rs_send.at[way, c, t], rs_recv.at[way, c, t], at_z(1 - 2 * way),
            )

    def rs_final(c):
        value = partial(c, z)
        for way in range(2):
            block = (way, 3, slice(None), cols(c))
            arrived(rs_in.at[block], rs_send.at[way, c, 3], rs_recv.at[way, c, 3])
        for at, mine in value:
            total = mine + (rs_in[0, 3, :, at, :].astype(F32) + rs_in[1, 3, :, at, :].astype(F32))
            spec[:, at, :] = total.astype(BF16)
        for k in range(1, Q):
            other = (q + k) % Q
            send(
                spec.at[pl.ds(other * 2, 2), cols(c), :], xs.at[CHUNKS[c][0], x, :, rows_of(c, q), :],
                c_send.at[c, k], c_recv.at[c, k], at_q(other),
            )
        xs[CHUNKS[c][0], x, :, rows_of(c, q), :] = spec[pl.ds(q * 2, 2), cols(c), :]

    def gather_first(c):
        for k in range(1, Q):
            other = (q - k + Q) % Q
            arrived(xs.at[CHUNKS[c][0], x, :, rows_of(c, other), :], c_send.at[c, k], c_recv.at[c, k])
        for way in range(2):
            block = xs.at[CHUNKS[c][0], x, :, rows(c), :]
            send(block, block, x_send.at[0, way, c], x_recv.at[0, way, c], at_x(1 - 2 * way))

    def spectrum(c, sources):
        parts = []
        for source in sources:
            real = xs[CHUNKS[c][0], source, 0, rows(c), :].astype(F32)
            imag = xs[CHUNKS[c][0], source, 1, rows(c), :].astype(F32)
            parts += [pack(real, swap(imag)), pack(-imag, swap(real))]
            parts += [pack(swap(real), imag), pack(-swap(imag), real)]
        return jnp.concatenate([part.astype(BF16) for part in parts], axis=0)

    def factors(c, sources, to):
        _, first, w = CHUNKS[c]
        parts = []
        for source in sources:
            for bottom in range(2):
                at = source * PATCHES + bottom * PAIRS + first * Q
                if not isinstance(source, int):
                    at = pl.multiple_of(at, C)
                parts += [factor[part, to, pl.ds(at, w * Q)] for part in range(2)]
        return wide(parts)

    def reflect(c, sources):
        h = CHUNKS[c][0]
        fresh = h not in begun
        begun.append(h)
        right = spectrum(c, sources)

        def body(b, _):
            to = pl.ds(pl.multiple_of(b * 256, 256), 256)
            value = jnp.dot(factors(c, sources, to), right, preferred_element_type=F32)
            acc[h, to, :] = value if fresh else acc[h, to, :] + value
            return 0

        lax.fori_loop(0, PATCHES // 256, body, 0)

    def gather_second(c):
        sides = [(x + X - 1) % X, (x + 1) % X]
        for way, source in enumerate(sides):
            block = xs.at[CHUNKS[c][0], source, :, rows(c), :]
            arrived(block, x_send.at[0, way, c], x_recv.at[0, way, c])
            block = xs.at[CHUNKS[c][0], source, way, rows(c), :]
            send(block, block, x_send.at[1, way, c], x_recv.at[1, way, c], at_x(1 - 2 * way))
        if c == 0:
            load.wait()
        if c in LAST:
            reflect(c, [x] + sides)

    def gather_third(c):
        source = (x + 2) % X
        for way in range(2):
            block = xs.at[CHUNKS[c][0], source, way, rows(c), :]
            arrived(block, x_send.at[1, way, c], x_recv.at[1, way, c])
        if c not in LAST:
            reflect(c, range(X))
            return
        h = CHUNKS[c][0]
        right = spectrum(c, [source])
        for b in range(FIRST[h], c + 1):
            both = []
            for bottom in range(2):
                to = rows(b, bottom)
                value = jnp.dot(factors(c, [source], to), right, preferred_element_type=F32)
                both.append(acc[h, to, :] + value)
            top, bottom = both
            refl[h, 0, rows(b), :] = pack(top, swap(bottom)).astype(BF16)
            refl[h, 1, rows(b), :] = pack(swap(top), bottom).astype(BF16)
            for k in range(1, Q):
                other = (q + k) % Q
                send(
                    refl.at[h, :, rows_of(b, other), :], gath.at[z, pl.ds(q * 2, 2), cols(b), :],
                    d_send.at[b, k], d_recv.at[b, k], at_q(other),
                )
            gath[z, pl.ds(q * 2, 2), cols(b), :] = refl[h, :, rows_of(b, q), :]

    def ag_step(c, t):
        if t == 0:
            for k in range(1, Q):
                other = (q - k + Q) % Q
                arrived(
                    gath.at[z, pl.ds(other * 2, 2), cols(c), :], d_send.at[c, k], d_recv.at[c, k]
                )
        for way in range(2):
            source = (z - t + Z) % Z if way == 0 else (z + t) % Z
            block = gath.at[source, :, cols(c), :]
            if t > 0:
                arrived(block, g_send.at[way, c, t - 1], g_recv.at[way, c, t - 1])
            if t == 3:
                block = gath.at[source, pl.ds(way * half, half), cols(c), :]
            send(block, block, g_send.at[way, c, t], g_recv.at[way, c, t], at_z(1 - 2 * way))

    def irradiance_out(c):
        for way in range(2):
            block = gath.at[(z + 4) % Z, pl.ds(way * half, half), cols(c), :]
            arrived(block, g_send.at[way, c, 3], g_recv.at[way, c, 3])
        right = wide([gath[:, :, t, :].reshape(Z * RT, C) for t in tiles(c)])
        count = 2 * S * T
        for k in range(Y):
            other = (y + k) % Y
            left = ik[pl.ds(pl.multiple_of(other * count, count), count), :]
            value = jnp.dot(left, right, preferred_element_type=F32).astype(BF16)
            for g, t in enumerate(tiles(c)):
                irr_out[pl.ds(other * 2 * S, 2 * S), t, :] = (
                    value[:, g * C : (g + 1) * C].reshape(2 * S, T, C)
                )
            for j in range(CORES):
                if k == 0 and j == 0:
                    continue
                to = other * CORES + (core + j) % CORES
                n = k * CORES + j
                send(
                    irr_out.at[pl.ds(to * S, S), cols(c), :], irr.at[CHUNKS[c][0], :, rows_of(c, q), :],
                    h_send.at[c, n], h_recv.at[c, n], at_q(to),
                )
        irr[CHUNKS[c][0], :, rows_of(c, q), :] = irr_out[pl.ds(q * S, S), cols(c), :]

    def finish(c):
        for k in range(Y):
            for j in range(CORES):
                if k == 0 and j == 0:
                    continue
                source = ((y - k + Y) % Y) * CORES + (core + j) % CORES
                n = k * CORES + j
                arrived(irr.at[CHUNKS[c][0], :, rows_of(c, source), :], h_send.at[c, n], h_recv.at[c, n])
        h = CHUNKS[c][0]
        rest = 1.0 - emission[rows(c), :]

        def body(s, _):
            value = irr[h, s, rows(c), :].astype(F32)
            value = emitted[h, s, rows(c), :].astype(F32) + rest * value
            if h == 0:
                irr[0, s, rows(c), :] = value.astype(BF16)
            else:
                other = irr[0, s, rows(c), :].astype(F32)
                out[s, rows(c), :] = pack(other, swap(value)).astype(BF16)
                out[s, rows(c, 1), :] = pack(swap(other), value).astype(BF16)
            return 0

        lax.fori_loop(0, S, body, 0)

    def start(c):
        emit(c)
        stations_out(c)

    absorb()
    pl.semaphore_wait(barrier, len(peers))
    stages = [start] + [functools.partial(rs_step, t=t) for t in range(4)]
    stages += [rs_final, gather_first, gather_second, gather_third]
    stages += [functools.partial(ag_step, t=t) for t in range(4)] + [irradiance_out, finish]
    done = [0] * NC
    ready = False
    for c in ORDER:
        if done[c] == 1 and not ready:
            transforms()
            ready = True
        stages[done[c]](c)
        done[c] += 1
    for op in sent:
        op.wait_send()


def local(emissive, classes, emissivity, mode_ids, view_factor):
    vmem = pl.BlockSpec(memory_space=pltpu.VMEM)
    dma = pltpu.SemaphoreType.DMA
    return pl.pallas_call(
        kernel,
        out_shape=jax.ShapeDtypeStruct(emissive.shape, BF16),
        in_specs=[vmem] * 4 + [pl.BlockSpec(memory_space=pl.ANY)],
        out_specs=vmem,
        scratch_shapes=[
            pltpu.VMEM((PAIRS, C), F32),
            pltpu.VMEM((Z * R, SZ * T), F32),
            pltpu.VMEM((SZ, Z * RT), F32),
            pltpu.VMEM((Z * RT, SZ * T), BF16),
            pltpu.VMEM((SZ * T, Z * RT), BF16),
            pltpu.VMEM((2, PATCHES, X * PATCHES), BF16),
            pltpu.VMEM((2, S, PAIRS, C), BF16),
            pltpu.VMEM((SZ, 2 * W, C), BF16),
            pltpu.VMEM((2, 4, R, 2 * W, C), BF16),
            pltpu.VMEM((2, 4, R, 2 * W, C), BF16),
            pltpu.VMEM((R, 2 * W, C), BF16),
            pltpu.VMEM((2, X, 2, PAIRS, C), BF16),
            pltpu.VMEM((2, PATCHES, C), F32),
            pltpu.VMEM((2, 2, PAIRS, C), BF16),
            pltpu.VMEM((Z, R, 2 * W, C), BF16),
            pltpu.VMEM((SZ, 2 * W, C), BF16),
            pltpu.VMEM((2, S, PAIRS, C), BF16),
            dma,
            dma((NC, Q)), dma((NC, Q)),
            dma((2, NC, 4)), dma((2, NC, 4)),
            dma((NC, Q)), dma((NC, Q)),
            dma((2, 2, NC)), dma((2, 2, NC)),
            dma((NC, Q)), dma((NC, Q)),
            dma((2, NC, 4)), dma((2, NC, 4)),
            dma((NC, Q)), dma((NC, Q)),
        ],
        compiler_params=pltpu.CompilerParams(
            collective_id=0, has_side_effects=True, vmem_limit_bytes=56 * 2**20
        ),
    )(emissive, classes[None, :], emissivity, mode_ids[None, :], view_factor[0])


def solution(mesh):
    placed = (P("mode", "blk", None), P("blk"), P(), P(), P("mode", None, "blk", None))
    return jax.shard_map(
        local, mesh=mesh, in_specs=placed, out_specs=P("mode", "blk", None), check_vma=False
    )
```

time: 141 us -> 119 us (0.84)
  Pallas kernels: 128 us -> 115 us
  other arithmetic: 7.37 us -> 0 us
  local copies, waits for them, and re-layouts: 5.86 us -> 3.93 us
    pallas_call x1, Pallas kernels: 128 us -> 115 us  [local(): pl.pallas_call(kernel, out_shape=jax.ShapeDtypeStruct(emissive.shape, BF1...]
    reduce_sum x1 -> x0, other arithmetic: 4.97 us -> none  [local(): emission = jnp.sum(jnp.where(pick[:, :, None], rates[None], 0.0), axis=1)]
    reshape x3 -> x0, local copies, waits for them, and re-layouts: 2.19 us -> none  [the longest x1 1.13 us: local(): itab = jnp.repeat(inverse.T, T, axis=1)]
where the time goes in v2:
time: 119 us
  Pallas kernels  115 us (97%)
  local copies, waits for them, and re-layouts  3.93 us (3%)
    pallas_call x1, Pallas kernels, local(): pl.pallas_call(kernel, out_shape=jax.ShapeDtypeStruct(emissive.shape, BF1...  115 us
    unnamed x1, local copies, waits for them, and re-layouts  2.66 us

profile of v2, /device:TPU:1, one launch (start us, length us, event | category | flops | bytes accessed | tf_op | source)
XLA Modules:
  0.0 118.9 jit_solution(6892167822901171012)
XLA Ops:
  0.0 1.3 %broadcast_in_dim.6.classes = s32[1,768]{1,0:T(1,128)} reshape(s32[768]{0:T(1024)} %param.6) | data formatting | bytes 6144 | tf_op jit(solution)/shard_map/broadcast_in_dim | solution.py:458
  1.3 114.9 %shard_map.55 = bf16[8,768,128]{2,1,0:T(8,128)(2,1)} custom-call(bf16[8,768,128]{2,1,0:T(8,128)(2,1)} %emissive.1, s32[1,768]{1,0:T(1,128)} %broadcast_in_dim.6.classes, f32[8,8]{1,0:T(8,128)} %emissivity.1, s32[1,64]{1,0:T(1,128)} %bitcast.3, bf16[2,768,3072]{2,1,0:T(8,128)(2,1)} %bitcast.2), custom_call_target="tpu_custom_call" | custom-call | tf_op jit(solution)/shard_map/pallas_call | solution.py:423
  116.2 2.7 %copy.7 = bf16[8,768,128]{2,1,0:T(8,128)(2,1)} copy(bf16[8,768,128]{2,1,0:T(8,128)(2,1)} %shard_map.55) | data formatting | bytes 3145728

commit v3 on v2

--- a/solution.py
+++ b/solution.py
@@ -15,7 +15,7 @@
 SZ = S * Q
 T = 16
 L = 64
-HALVES = ((16, 32), (16, 16, 16))
+HALVES = ((16, 32), (16, 32))
 CHUNKS = tuple((h, sum(ws[:n]), w) for h, ws in enumerate(HALVES) for n, w in enumerate(ws))
 NC = len(CHUNKS)
 FIRST = tuple(n for n, c in enumerate(CHUNKS) if c[1] == 0)
@@ -31,9 +31,8 @@
 F32, BF16 = jnp.float32, jnp.bfloat16
 HIGHEST = lax.Precision.HIGHEST
 ORDER = (
-    0, 1, 0, 3, 4, 0, 1, 0, 1, 4, 0, 1, 2, 1, 0, 2, 4, 1, 3, 0, 2, 4, 0, 3, 1, 2, 4, 0, 3, 1,
-    3, 1, 2, 3, 4, 0, 2, 1, 3, 4, 2, 0, 1, 3, 4, 2, 0, 3, 1, 2, 4, 0, 1, 2, 4, 3, 1, 2, 4, 3,
-    0, 2, 4, 2, 4, 3, 2, 3, 4, 0, 3, 1, 2, 4, 3,
+    0, 1, 0, 2, 0, 1, 3, 0, 1, 0, 2, 1, 0, 3, 2, 0, 1, 0, 3, 1, 2, 3, 0, 2, 1, 3, 1, 2, 1, 3,
+    2, 0, 2, 0, 3, 1, 2, 0, 3, 1, 3, 0, 1, 2, 3, 2, 0, 1, 3, 1, 2, 3, 2, 3, 2, 0, 3, 1, 2, 3,
 )
 
 
@@ -70,7 +69,7 @@
 
 def kernel(
     emissive, classes, emissivity, mode_ids, factor_hbm, out,
-    emission, ftab, itab, fk, ik, factor, emitted, station, rs_out, rs_in, spec, xs, acc, refl,
+    emission, ftab, itab, fk, ik, factor, emitted, station, terms, rs_out, rs_in, spec, xs, acc, refl,
     gath, irr_out, irr,
     f_sem, a_send, a_recv, rs_send, rs_recv, c_send, c_recv, x_send, x_recv,
     d_send, d_recv, g_send, g_recv, h_send, h_recv,
@@ -193,41 +192,51 @@
     def wide(parts):
         return parts[0] if len(parts) == 1 else jnp.concatenate(parts, axis=1)
 
-    def partial(c, target):
+    def partial(c, left):
         right = wide([station[:, t, :].reshape(SZ * T, C) for t in tiles(c)])
-        left = fk[pl.ds(pl.multiple_of(target * RT, RT), RT), :]
         value = jnp.dot(left, right, preferred_element_type=F32)
         return [
-            (t, value[:, g * C : (g + 1) * C].reshape(R, T, C)) for g, t in enumerate(tiles(c))
+            (t, value[:, g * C : (g + 1) * C].reshape(-1, R, T, C)) for g, t in enumerate(tiles(c))
         ]
+
+    def partials(c):
+        def body(b, _):
+            left = fk[pl.ds(pl.multiple_of(b * 2 * RT, 2 * RT), 2 * RT), :]
+            for t, value in partial(c, left):
+                terms[pl.ds(b * 2, 2), :, t, :] = value
+            return 0
+
+        lax.fori_loop(0, Z // 2, body, 0)
 
     half = R // 2
 
     def rs_step(c, t):
         if t == 0:
             stations_in(c)
-            value = partial(c, (z + 4) % Z)
+            far = (z + 4) % Z
+            value = partial(c, fk[pl.ds(pl.multiple_of(far * RT, RT), RT), :])
             for way in range(2):
                 hit = slice(way * half, (way + 1) * half)
                 for at, mine in value:
-                    rs_out[way, 0, hit, at, :] = mine[hit].astype(BF16)
+                    rs_out[way, 0, hit, at, :] = mine[0, hit].astype(BF16)
                 block = (way, 0, pl.ds(way * half, half), cols(c))
                 send(
                     rs_out.at[block], rs_in.at[block],
                     rs_send.at[way, c, 0], rs_recv.at[way, c, 0], at_z(1 - 2 * way),
                 )
+            partials(c)
             return
         for way in range(2):
-            value = partial(c, (z + 4 - t) % Z if way == 0 else (z + 4 + t) % Z)
+            target = (z + 4 - t) % Z if way == 0 else (z + 4 + t) % Z
             hit = slice(way * half, (way + 1) * half) if t == 1 else slice(0, R)
             miss = slice((1 - way) * half, (2 - way) * half)
             block = (way, t - 1, pl.ds(hit.start, hit.stop - hit.start), cols(c))
             arrived(rs_in.at[block], rs_send.at[way, c, t - 1], rs_recv.at[way, c, t - 1])
-            for at, mine in value:
-                total = mine[hit] + rs_in[way, t - 1, hit, at, :].astype(F32)
+            for at in tiles(c):
+                total = terms[target, hit, at, :] + rs_in[way, t - 1, hit, at, :].astype(F32)
                 rs_out[way, t, hit, at, :] = total.astype(BF16)
                 if t == 1:
-                    rs_out[way, t, miss, at, :] = mine[miss].astype(BF16)
+                    rs_out[way, t, miss, at, :] = terms[target, miss, at, :].astype(BF16)
             block = (way, t, slice(None), cols(c))
             send(
                 rs_out.at[block], rs_in.at[block],
@@ -235,12 +244,11 @@
             )
 
     def rs_final(c):
-        value = partial(c, z)
         for way in range(2):
             block = (way, 3, slice(None), cols(c))
             arrived(rs_in.at[block], rs_send.at[way, c, 3], rs_recv.at[way, c, 3])
-        for at, mine in value:
-            total = mine + (rs_in[0, 3, :, at, :].astype(F32) + rs_in[1, 3, :, at, :].astype(F32))
+        for at in tiles(c):
+            total = terms[z, :, at, :] + (rs_in[0, 3, :, at, :].astype(F32) + rs_in[1, 3, :, at, :].astype(F32))
             spec[:, at, :] = total.astype(BF16)
         for k in range(1, Q):
             other = (q + k) % Q
@@ -434,6 +442,7 @@
             pltpu.VMEM((2, PATCHES, X * PATCHES), BF16),
             pltpu.VMEM((2, S, PAIRS, C), BF16),
             pltpu.VMEM((SZ, 2 * W, C), BF16),
+            pltpu.VMEM((Z, R, 2 * W, C), F32),
             pltpu.VMEM((2, 4, R, 2 * W, C), BF16),
             pltpu.VMEM((2, 4, R, 2 * W, C), BF16),
             pltpu.VMEM((R, 2 * W, C), BF16),
@@ -453,7 +462,7 @@
             dma((NC, Q)), dma((NC, Q)),
         ],
         compiler_params=pltpu.CompilerParams(
-            collective_id=0, has_side_effects=True, vmem_limit_bytes=56 * 2**20
+            collective_id=0, has_side_effects=True, vmem_limit_bytes=50 * 2**20
         ),
     )(emissive, classes[None, :], emissivity, mode_ids[None, :], view_factor[0])
 

time: 119 us -> 116 us (0.975)
  Pallas kernels: 115 us -> 112 us
    pallas_call x1, Pallas kernels: 115 us -> 112 us  [local(): pl.pallas_call(kernel, out_shape=jax.ShapeDtypeStruct(emissive.shape, BF1...]
    unnamed x1 -> x7, local copies, waits for them, and re-layouts: 2.66 us -> 3.89 us
where the time goes in v3:
time: 116 us
  Pallas kernels  112 us (97%)
  local copies, waits for them, and re-layouts  4.58 us (4%)
    pallas_call x1, Pallas kernels, local(): pl.pallas_call(kernel, out_shape=jax.ShapeDtypeStruct(emissive.shape, BF1...  112 us
    unnamed x7, local copies, waits for them, and re-layouts  3.89 us

profile of v3, /device:TPU:1, one launch (start us, length us, event | category | flops | bytes accessed | tf_op | source)
XLA Modules:
  0.0 116.3 jit_solution(5944172802400886455)
XLA Ops:
  0.0 0.7 broadcast_in_dim.6.classes
  0.7 0.0 copy-start
  0.7 1.4 %copy-done = bf16[8,768,128]{2,1,0:T(8,128)(2,1)S(1)} copy-done((bf16[8,768,128]{2,1,0:T(8,128)(2,1)S(1)}, bf16[8,768,128]{2,1,0:T(8,128)(2,1)}, u32[]{:S(2)}) %copy-start) | copy-done | bytes 1572888
  2.1 0.0 copy-start.1
  2.1 0.7 copy-done.1
  2.8 0.0 copy-start.2
  2.8 0.7 copy-done.2
  3.4 111.7 %shard_map.55 = bf16[8,768,128]{2,1,0:T(8,128)(2,1)S(1)} custom-call(bf16[8,768,128]{2,1,0:T(8,128)(2,1)S(1)} %copy-done, s32[1,768]{1,0:T(1,128)S(1)} %broadcast_in_dim.6.classes, f32[8,8]{1,0:T(8,128)S(1)} %copy-done.1, s32[1,64]{1,0:T(1,128)S(1)} %bitcast.2, bf16[2,768,3072]{2,1,0:T(8,128)(2,1)} %bitcast.3), custom_call_target="tpu_custom_call" | custom-call | tf_op jit(solution)/shard_map/pallas_call | solution.py:431
  115.1 1.1 copy.7
Async XLA Ops:
  0.7 1.4 %copy-start = (bf16[8,768,128]{2,1,0:T(8,128)(2,1)S(1)}, bf16[8,768,128]{2,1,0:T(8,128)(2,1)}, u32[]{:S(2)}) copy-start(bf16[8,768,128]{2,1,0:T(8,128)(2,1)} %emissive.1) | copy-start | bytes 4718596
  2.1 0.7 copy-start.1
  2.8 0.7 copy-start.2
